TPU v7x, 1024 devices: a whole 4x8x16 slice. The times are simulated.
1024 devices in a mesh: section: 16 (over y, x_lo), replica: 64 (over z, x_hi, core).
Axes of the slice: x: 4 (x_hi: 2, x_lo: 2; x = x_hi * 2 + x_lo), y: 8, z: 16, core: 2. Of those that a mesh axis runs over, the one named last changes fastest.
Arguments:
- hidden: bfloat16 [16, 16384, 64], P('section', 'replica'), may hold values from -16 to 16
- out_grad: bfloat16 [16, 16384, 6144], P('section', 'replica'), may hold values from -6 to 6
- weights_old: bfloat16 [1024, 6144], P('section'), may hold values from -6 to 6
- master: float32 [1024, 6144], P(('section', 'replica')), may hold values from -6 to 6
- first_moment: float32 [1024, 6144], P(('section', 'replica')), may hold values from -4 to 4
- second_moment: float32 [1024, 6144], P(('section', 'replica')), may hold values from 0.01 to 1
- owner_order: int32 [64], replicated, may hold values from 0 to 63, each once
- step_count: int32 [1], replicated, may hold values from 1 to 8
Outputs:
- new_master: float32 [1024, 6144], P(('section', 'replica'))
- new_first: float32 [1024, 6144], P(('section', 'replica'))
- new_second: float32 [1024, 6144], P(('section', 'replica'))
- checkpoint: float32 [3, 1024, 6144], P(None, ('section', 'replica'))
- weights_new: bfloat16 [1024, 6144], P('section')
- hidden_grad: bfloat16 [16, 16384, 64], P('section', 'replica')
Inputs may be any that keep to these rules, and one draw needn't show every extreme that they name: Replica r owns block owner_order[r] of its section's bucket.
All inputs are finite; a program needn't handle non-finite values.
Results may differ from a plain program's by a relative error of at most 0.005.
Values may be sent and summed in bfloat16 or wider, within the bound.
A program may use at most 32 MiB of HBM per device.

v0:
```python
import jax
import jax.numpy as jnp
from jax import lax
from jax.sharding import PartitionSpec as P


def cut_along(array, dim, devices):
    before, after = (array.shape[:dim], array.shape[dim + 1 :])
    return jnp.moveaxis(array.reshape(*before, devices, -1, *after), dim, 0)


def sent_and_summed(array, axis, dim):
    devices = lax.axis_size(axis)
    blocks = lax.all_to_all(cut_along(array, dim, devices), axis, 0, 0, tiled=True)
    return jnp.sum(blocks, axis=0)


def passed_along(array, axis, by):
    devices = lax.axis_size(axis)
    return lax.ppermute(array, axis, [(i, (i + by) % devices) for i in range(devices)])


def from_everyone(array, axis):
    copies = jnp.broadcast_to(array, (lax.axis_size(axis), *array.shape))
    return lax.all_to_all(copies, axis, split_axis=0, concat_axis=0, tiled=True)


def laid_out(blocks, dim):
    dims = list(blocks.shape[1:])
    dims[dim] *= blocks.shape[0]
    return jnp.moveaxis(blocks, 0, dim).reshape(dims)


def collect(array, axis, dim):
    blocks = from_everyone(array, axis)
    return laid_out(blocks, dim)


def adam_update(grads, master, first, second, steps):
    first_new = 0.9 * first + 0.1 * grads
    second_new = 0.95 * second + 0.05 * grads * grads
    fix_one = 1.0 - jnp.power(0.9, steps)
    fix_two = 1.0 - jnp.power(0.95, steps)
    update = first_new / fix_one / (jnp.sqrt(second_new / fix_two) + 1e-08)
    master_new = master - 0.05 * (update + 0.1 * master)
    return (master_new, first_new, second_new)


def per_device(
    hidden, out_grad, weights_old, master, first_moment, second_moment, owner_order, step_count
):
    replicas = lax.axis_size("replica")
    block = master.shape[0]
    slab_rows = weights_old.shape[0]
    width = out_grad.shape[2]
    acts = hidden[0]
    grads_out = out_grad[0]
    tokens = acts.shape[0]
    acts_blocks = acts.reshape(tokens, replicas, block)
    steps = step_count[0].astype(jnp.float32)
    columns = jnp.take(acts_blocks, owner_order, axis=1).reshape(tokens, slab_rows)
    product = lax.dot_general(
        columns, grads_out, (((0,), (0,)), ((), ())), preferred_element_type=jnp.float32
    )
    full_term = product / tokens
    owned = sent_and_summed(full_term, "replica", 0)
    back = lax.dot_general(
        grads_out, weights_old, (((1,), (1,)), ((), ())), preferred_element_type=jnp.float32
    )
    hidden_grad = (back * width ** (-0.5)).astype(jnp.bfloat16)
    new_master, new_first, new_second = adam_update(
        owned, master, first_moment, second_moment, steps
    )
    moved = passed_along((new_master, new_first, new_second), "replica", 1)
    checkpoint = jnp.stack([moved[0], moved[1], moved[2]])
    gathered = collect(new_master.astype(jnp.bfloat16), "replica", 0)
    inverse = (
        jnp.zeros((replicas,), jnp.int32).at[owner_order].set(jnp.arange(replicas, dtype=jnp.int32))
    )
    weights_new = jnp.take(gathered.reshape(replicas, block, width), inverse, axis=0).reshape(
        slab_rows, width
    )
    return (new_master, new_first, new_second, checkpoint, weights_new, hidden_grad[None])


def solution(mesh):
    placed = (
        P("section", "replica", None),
        P("section", "replica", None),
        P("section", None),
        P(("section", "replica"), None),
        P(("section", "replica"), None),
        P(("section", "replica"), None),
        P(),
        P(),
    )
    return jax.shard_map(
        per_device,
        mesh=mesh,
        in_specs=placed,
        out_specs=(
            P(("section", "replica"), None),
            P(("section", "replica"), None),
            P(("section", "replica"), None),
            P(None, ("section", "replica"), None),
            P("section", None),
            P("section", "replica", None),
        ),
        check_vma=False,
    )
```

profile of v0, /device:TPU:1, one launch (start us, length us, event | category | flops | bytes accessed | tf_op | source)
XLA Modules:
  0.0 188.6 jit_solution(6153636430513649755)
XLA Ops:
  0.6 0.0 copy-start
  0.6 0.8 compare_select_fusion.1
  1.5 0.8 compare_and_fusion.1
  2.3 1.4 gather_fusion
  3.7 0.0 copy-done
  3.7 0.7 fusion
  4.4 2.8 %copy.15 = f32[64,1,6144]{2,1,0:T(1,128)} copy(f32[64,1,6144]{2,0,1:T(8,128)S(1)} %fusion) | data formatting | bytes 3145728 | tf_op jit(solution)/shard_map/reshape | solution.py:9
  7.2 23.4 %all-to-all-start = ((f32[64,1,6144]{2,1,0:T(1,128)}), f32[64,1,6144]{2,1,0:T(1,128)}, u32[]{:S(2)}, u32[]{:S(2)}) async-start(f32[64,1,6144]{2,1,0:T(1,128)} %copy.15), calls=%async_computation | async-start | bytes 3145728 | tf_op jit(solution)/shard_map/all_to_all | solution.py:14
  30.6 0.0 copy-start.1
  30.7 0.0 copy-start.2
  30.7 0.0 copy-start.3
  31.4 75.6 %all-to-all-done = f32[64,1,6144]{2,1,0:T(1,128)} async-done(((f32[64,1,6144]{2,1,0:T(1,128)}), f32[64,1,6144]{2,1,0:T(1,128)}, u32[]{:S(2)}, u32[]{:S(2)}) %all-to-all-start) | async-done | bytes 1572896 | tf_op jit(solution)/shard_map/all_to_all | solution.py:14
  107.0 2.4 %reduce_sum.11 = f32[6144]{0:T(1024)S(1)} reduce(f32[64,1,6144]{2,1,0:T(1,128)} %all-to-all-done, f32[]{:T(128)} %constant.29.clone.1), dimensions={0,1}, to_apply=%region_0.1 | reduce | flops 387072 | bytes 1597444 | tf_op jit(solution)/shard_map/reduce_sum | solution.py:15
  109.4 0.0 copy-done.1
  109.4 0.0 copy-done.2
  109.4 0.0 copy-done.3
  109.4 0.2 convert_reduce_fusion
  109.7 0.0 copy-start.6
  109.7 0.0 copy-start.5
  109.7 0.0 copy-start.4
  109.7 2.0 %broadcast_in_dim.35 = bf16[64,1,6144]{2,1,0:T(2,128)(2,1)} broadcast(bf16[6144]{0:T(1024)(128)(2,1)S(1)} %get-tuple-element.6), dimensions={2} | broadcast | bytes 798720 | tf_op jit(solution)/shard_map/broadcast_in_dim | solution.py:24
  111.7 0.5 broadcast.87
  112.2 7.3 %reduce.3 = bf16[64,6144]{1,0:T(8,128)(2,1)} reduce(bf16[64,1,6144]{2,1,0:T(2,128)(2,1)} %broadcast_in_dim.35, bf16[]{:T(256)} %broadcast.87), dimensions={1}, to_apply=%broadcast_in_dim.35.reduce_sub_computation | reduce | bytes 1572866 | tf_op jit(solution)/shard_map/broadcast_in_dim | solution.py:24
  119.5 3.2 %reshape.146 = bf16[64,2,3072]{2,1,0:T(2,128)(2,1)} reshape(bf16[64,6144]{1,0:T(8,128)(2,1)} %reduce.3) | data formatting | bytes 1572864
  122.7 7.8 %all-to-all-start.1 = ((bf16[64,2,3072]{2,1,0:T(2,128)(2,1)}), bf16[64,2,3072]{2,1,0:T(2,128)(2,1)}, u32[]{:S(2)}, u32[]{:S(2)}) async-start(bf16[64,2,3072]{2,1,0:T(2,128)(2,1)} %reshape.146), calls=%async_computation.1 | async-start | bytes 1572864 | tf_op jit(solution)/shard_map/all_to_all | solution.py:25
  130.6 0.8 scatter_custom_fusion
  131.4 2.8 %fusion.10 = bf16[1,256,64]{1,2,0:T(8,128)(2,1)} fusion(bf16[64,6144]{1,0:T(8,128)(2,1)} %param.10, bf16[1,256,6144]{2,1,0:T(8,128)(2,1)S(1)} %copy-done), kind=kOutput, calls=%fused_computation.10 | convolution fusion | flops 201359360 | bytes 3964928 | tf_op jit(solution)/shard_map/dot_general | solution.py:67
  134.2 0.0 copy-done.6
  134.2 5.0 %collective-permute-start.1 = (f32[1,6144]{1,0:T(1,128)S(1)}, f32[1,6144]{1,0:T(1,128)S(1)}, u32[]{:S(2)}, u32[]{:S(2)}) collective-permute-start(f32[1,6144]{1,0:T(1,128)S(1)} %get-tuple-element.9), channel_id=1, source_target_pairs={{0,1},{1,2},{2,3},{3,4},{4,5},{5,6},{6,7},{7,8},{8,9},{9,10},{10,1... | collective-permute-start | bytes 73736 | tf_op jit(solution)/shard_map/ppermute | solution.py:20
  139.3 0.0 copy-done.5
  139.3 2.1 %collective-permute-start.2 = (f32[1,6144]{1,0:T(1,128)S(1)}, f32[1,6144]{1,0:T(1,128)S(1)}, u32[]{:S(2)}, u32[]{:S(2)}) collective-permute-start(f32[1,6144]{1,0:T(1,128)S(1)} %get-tuple-element.8), channel_id=1, source_target_pairs={{0,1},{1,2},{2,3},{3,4},{4,5},{5,6},{6,7},{7,8},{8,9},{9,10},{10,1... | collective-permute-start | bytes 73736 | tf_op jit(solution)/shard_map/ppermute | solution.py:20
  141.3 0.0 copy-done.4
  141.3 3.3 %collective-permute-start = (f32[1,6144]{1,0:T(1,128)S(1)}, f32[1,6144]{1,0:T(1,128)S(1)}, u32[]{:S(2)}, u32[]{:S(2)}) collective-permute-start(f32[1,6144]{1,0:T(1,128)S(1)} %get-tuple-element.7), channel_id=1, source_target_pairs={{0,1},{1,2},{2,3},{3,4},{4,5},{5,6},{6,7},{7,8},{8,9},{9,10},{10,1... | collective-permute-start | bytes 73736 | tf_op jit(solution)/shard_map/ppermute | solution.py:20
  144.7 0.0 collective-permute-done.1
  144.7 0.0 collective-permute-done.2
  144.7 0.9 collective-permute-done
  145.6 0.7 pad_maximum_fusion
  146.3 27.8 %all-to-all-done.1 = bf16[64,2,3072]{2,1,0:T(2,128)(2,1)} async-done(((bf16[64,2,3072]{2,1,0:T(2,128)(2,1)}), bf16[64,2,3072]{2,1,0:T(2,128)(2,1)}, u32[]{:S(2)}, u32[]{:S(2)}) %all-to-all-start.1) | async-done | bytes 786464 | tf_op jit(solution)/shard_map/all_to_all | solution.py:25
  174.1 5.8 %reshape.147 = bf16[64,1,6144]{2,1,0:T(2,128)(2,1)} reshape(bf16[64,2,3072]{2,1,0:T(2,128)(2,1)} %all-to-all-done.1) | data formatting | bytes 1572864
  179.9 2.7 %copy.18 = bf16[64,1,6144]{2,0,1:T(8,128)(2,1)} copy(bf16[64,1,6144]{2,1,0:T(2,128)(2,1)} %reshape.147) | data formatting | bytes 1572864
  182.6 3.9 %gather_fusion.1 = bf16[64,6144]{1,0:T(8,128)(2,1)} fusion(bf16[64,6144]{1,0:T(8,128)(2,1)} %bitcast.36, s32[1024]{0:T(1024)S(1)} %pad_clamp_fusion), kind=kCustom, calls=%fused_computation.1 | custom fusion | bytes 1573120 | tf_op jit(solution)/shard_map/jit(_take)/gather | solution.py:80
  186.5 2.2 %broadcast_select_fusion = bf16[64,6144]{1,0:T(8,128)(2,1)} fusion(bf16[64,6144]{1,0:T(8,128)(2,1)} %gather_fusion.1, pred[64]{0:T(512)(128)(4,1)S(1)} %compare_and_fusion), kind=kLoop, calls=%fused_computation.12 | loop fusion | flops 393216 | bytes 1572928 | tf_op jit(solution)/shard_map/jit(_take)/select_n | solution.py:80
  (5 shorter events, 0.0 us)
Async XLA Ops:
  0.6 3.1 %copy-start = (bf16[1,256,6144]{2,1,0:T(8,128)(2,1)S(1)}, bf16[1,256,6144]{2,1,0:T(8,128)(2,1)}, u32[]{:S(2)}) copy-start(bf16[1,256,6144]{2,1,0:T(8,128)(2,1)} %param.9) | copy-start | bytes 9437188
  7.2 99.8 %all-to-all-start = ((f32[64,1,6144]{2,1,0:T(1,128)}), f32[64,1,6144]{2,1,0:T(1,128)}, u32[]{:S(2)}, u32[]{:S(2)}) async-start(f32[64,1,6144]{2,1,0:T(1,128)} %copy.15), calls=%async_computation | async-start | bytes 3145728 | tf_op jit(solution)/shard_map/all_to_all | solution.py:14
  30.6 78.8 %copy-start.1 = (f32[1,6144]{1,0:T(1,128)S(1)}, f32[1,6144]{1,0:T(1,128)}, u32[]{:S(2)}) copy-start(f32[1,6144]{1,0:T(1,128)} %param.11) | copy-start | bytes 73732
  30.7 78.8 %copy-start.2 = (f32[1,6144]{1,0:T(1,128)S(1)}, f32[1,6144]{1,0:T(1,128)}, u32[]{:S(2)}) copy-start(f32[1,6144]{1,0:T(1,128)} %param.13) | copy-start | bytes 73732
  30.7 78.8 %copy-start.3 = (f32[1,6144]{1,0:T(1,128)S(1)}, f32[1,6144]{1,0:T(1,128)}, u32[]{:S(2)}) copy-start(f32[1,6144]{1,0:T(1,128)} %param.12) | copy-start | bytes 73732
  109.7 24.6 %copy-start.6 = (f32[1,6144]{1,0:T(1,128)}, f32[1,6144]{1,0:T(1,128)S(1)}, u32[]{:S(2)}) copy-start(f32[1,6144]{1,0:T(1,128)S(1)} %get-tuple-element.9) | copy-start | bytes 73732
  109.7 29.6 %copy-start.5 = (f32[1,6144]{1,0:T(1,128)}, f32[1,6144]{1,0:T(1,128)S(1)}, u32[]{:S(2)}) copy-start(f32[1,6144]{1,0:T(1,128)S(1)} %get-tuple-element.8) | copy-start | bytes 73732
  109.7 31.6 %copy-start.4 = (f32[1,6144]{1,0:T(1,128)}, f32[1,6144]{1,0:T(1,128)S(1)}, u32[]{:S(2)}) copy-start(f32[1,6144]{1,0:T(1,128)S(1)} %get-tuple-element.7) | copy-start | bytes 73732
  122.7 51.4 %all-to-all-start.1 = ((bf16[64,2,3072]{2,1,0:T(2,128)(2,1)}), bf16[64,2,3072]{2,1,0:T(2,128)(2,1)}, u32[]{:S(2)}, u32[]{:S(2)}) async-start(bf16[64,2,3072]{2,1,0:T(2,128)(2,1)} %reshape.146), calls=%async_computation.1 | async-start | bytes 1572864 | tf_op jit(solution)/shard_map/all_to_all | solution.py:25
  134.2 10.5 %collective-permute-start.1 = (f32[1,6144]{1,0:T(1,128)S(1)}, f32[1,6144]{1,0:T(1,128)S(1)}, u32[]{:S(2)}, u32[]{:S(2)}) collective-permute-start(f32[1,6144]{1,0:T(1,128)S(1)} %get-tuple-element.9), channel_id=1, source_target_pairs={{0,1},{1,2},{2,3},{3,4},{4,5},{5,6},{6,7},{7,8},{8,9},{9,10},{10,1... | collective-permute-start | bytes 73736 | tf_op jit(solution)/shard_map/ppermute | solution.py:20
  139.3 5.4 %collective-permute-start.2 = (f32[1,6144]{1,0:T(1,128)S(1)}, f32[1,6144]{1,0:T(1,128)S(1)}, u32[]{:S(2)}, u32[]{:S(2)}) collective-permute-start(f32[1,6144]{1,0:T(1,128)S(1)} %get-tuple-element.8), channel_id=1, source_target_pairs={{0,1},{1,2},{2,3},{3,4},{4,5},{5,6},{6,7},{7,8},{8,9},{9,10},{10,1... | collective-permute-start | bytes 73736 | tf_op jit(solution)/shard_map/ppermute | solution.py:20
  141.3 4.3 %collective-permute-start = (f32[1,6144]{1,0:T(1,128)S(1)}, f32[1,6144]{1,0:T(1,128)S(1)}, u32[]{:S(2)}, u32[]{:S(2)}) collective-permute-start(f32[1,6144]{1,0:T(1,128)S(1)} %get-tuple-element.7), channel_id=1, source_target_pairs={{0,1},{1,2},{2,3},{3,4},{4,5},{5,6},{6,7},{7,8},{8,9},{9,10},{10,1... | collective-permute-start | bytes 73736 | tf_op jit(solution)/shard_map/ppermute | solution.py:20
where the time goes:
time: 190 us; the launch traced here: 189 us
  waiting for transfers between devices  104 us (55%)
  starting transfers between devices  41.7 us (22%)
  local copies, waits for them, and re-layouts  23.2 us (12%)
  other arithmetic  14.4 us (8%)
  matrix products  3.54 us (2%)
    all_to_all x1, waiting for transfers between devices, sent_and_summed(): lax.all_to_all(cut_along(array, dim, devices), axis, 0, 0, tiled=True)  75.6 us
    all_to_all x1, waiting for transfers between devices, from_everyone(): return lax.all_to_all(copies, axis, split_axis=0, concat_axis=0, tiled=True)  27.8 us
    all_to_all x1, starting transfers between devices, sent_and_summed(): lax.all_to_all(cut_along(array, dim, devices), axis, 0, 0, tiled=True)  23.4 us
    unnamed x17, local copies, waits for them, and re-layouts  11.8 us
    ppermute x3, starting transfers between devices, passed_along(): lax.ppermute(array, axis, [(i, (i + by) % devices) for i in range(devices)])  10.4 us
    all_to_all x1, starting transfers between devices, from_everyone(): return lax.all_to_all(copies, axis, split_axis=0, concat_axis=0, tiled=True)  7.84 us
    broadcast_in_dim x1, other arithmetic, from_everyone(): copies = jnp.broadcast_to(array, (lax.axis_size(axis), *array.shape))  7.28 us
    gather x1, local copies, waits for them, and re-layouts, per_device(): jnp.take(gathered.reshape(replicas, block, width), inverse, axis=0)  3.89 us
  transfers between devices with their start and end apart: 5, of which 3 were waited for; matrix products, arithmetic and copies ran while one was open for 2% of the time, Pallas kernels for 0%

commit v1 on v0

v1 whole, which is shorter than its diff:
```python
import jax
import jax.numpy as jnp
from jax import lax
from jax.experimental import pallas as pl
from jax.experimental.pallas import tpu as pltpu
from jax.sharding import PartitionSpec as P

MESH = pl.DeviceIdType.MESH
F32 = jnp.float32
BF16 = jnp.bfloat16

D = 6144
ROWS = 64
TOK = 256
CH = 3
W = D // CH
J = W // 128
FLIPS = [(i, f) for f in (1, 0) for i in range(4) if (i, f) != (0, 0)]


def rep_of(p):
    c, xh, zl, zh = p // 32, (p // 16) % 2, (p // 4) % 4, p % 4
    return (zh * 4 + zl) * 4 + xh * 2 + c


def kernel(
    hid_hbm, own_hbm, step_ref, og_hbm, w_hbm, m_hbm, f_hbm, s_hbm,
    nm_ref, nf_ref, ns_ref, ck_ref, wn_ref, hg_ref,
    hid_ref, own_ref, m_ref, f_ref, s_ref, og, w, part, core_in, full, t1, in1, acc1, t2, in2, ag, wide, moved,
    ld_sem, core_s, core_r, s1, r1, s2, r2, sa, ra, sb, rb, sc, rc, sk, rk,
):
    r = lax.axis_index("replica")
    z, xh, c = r // 4, (r // 2) % 2, r % 2
    a, zl = z // 4, z % 4
    g = xh * 4 + zl

    def rep(z_, x_, c_):
        return ((z_ + 32) % 16) * 4 + x_ * 2 + c_

    offs = [0, 1, -1, 2 - 4 * c]
    sib = rep(z, xh, 1 - c)
    nxt, prv = (r + 1) % 64, (r + 63) % 64
    near_to = [(rep(z + offs[i], (xh + f) % 2, c)) for i, f in FLIPS]
    near_from = [(rep(z - offs[i], (xh + f) % 2, c)) for i, f in FLIPS]
    far = [rep(z + 4 * d, xh, c) for d in (1, 2, 3)]

    def remote(src, dst, ssem, rsem, to):
        return pltpu.make_async_remote_copy(
            src_ref=src, dst_ref=dst, send_sem=ssem, recv_sem=rsem,
            device_id={"replica": to}, device_id_type=MESH,
        )

    loads = [
        pltpu.make_async_copy(own_hbm, own_ref, ld_sem.at[CH + 1]),
        pltpu.make_async_copy(hid_hbm, hid_ref, ld_sem.at[CH + 2]),
    ]
    for ch in range(CH):
        cols = pl.ds(ch * W, W)
        loads.append(pltpu.make_async_copy(og_hbm.at[:, cols], og.at[:, cols], ld_sem.at[ch]))
    loads += [
        pltpu.make_async_copy(w_hbm, w, ld_sem.at[CH]),
        pltpu.make_async_copy(m_hbm, m_ref, ld_sem.at[CH + 3]),
        pltpu.make_async_copy(f_hbm, f_ref, ld_sem.at[CH + 4]),
        pltpu.make_async_copy(s_hbm, s_ref, ld_sem.at[CH + 5]),
    ]
    for x in loads:
        x.start()

    barrier = pltpu.get_barrier_semaphore()
    for to in [sib, prv] + near_from + far:
        pl.semaphore_signal(barrier, inc=1, device_id={"replica": to}, device_id_type=MESH)

    loads[0].wait()
    loads[1].wait()
    k_i = lax.broadcasted_iota(jnp.int32, (ROWS, ROWS), 0)
    p_i = lax.broadcasted_iota(jnp.int32, (ROWS, ROWS), 1)
    owns = jnp.where(own_ref[...] == k_i, 1.0, 0.0).astype(BF16)
    places = jnp.where(k_i == rep_of(p_i), 1.0, 0.0).astype(BF16)
    at = jnp.dot(owns, places, preferred_element_type=F32).astype(BF16)
    hid = lax.dot_general(
        at, hid_ref[...], (((0,), (0,)), ((), ())), preferred_element_type=F32
    ).astype(BF16)

    sends = []

    def start(copy):
        copy.start()
        sends.append(copy)
        return copy

    mine = pl.ds(pl.multiple_of(c * 32, 32), 32)
    theirs = pl.ds(pl.multiple_of((1 - c) * 32, 32), 32)
    core = []
    for ch in range(CH):
        loads[2 + ch].wait()
        for n in range(W // 512):
            at_col = ch * W + n * 512
            part[ch, :, n * 512 : (n + 1) * 512] = jnp.dot(
                hid, og[:, at_col : at_col + 512], preferred_element_type=F32
            )
        if ch == 0:
            pl.semaphore_wait(barrier, 12)
        core.append(
            start(remote(part.at[ch, theirs], core_in.at[ch], core_s.at[ch], core_r.at[ch], sib))
        )

    near = []
    for ch in range(CH):
        core[ch].wait_recv()
        for j in range(J):
            lanes = pl.ds(j * 128, 128)
            full[ch, pl.ds(j, 32, stride=J), :] = part[ch, mine, lanes] + core_in[ch, :, lanes]
        t1[ch] = full[ch].astype(BF16)
        row = []
        for k, (i, f) in enumerate(FLIPS):
            there = ((xh + f) % 2) * 4 + (z + offs[i] + 16) % 4
            src = t1.at[ch, pl.ds(pl.multiple_of(there * 4 * J, 64), 4 * J)]
            row.append(start(remote(src, in1.at[ch, k], s1.at[ch, k], r1.at[ch, k], near_to[k])))
        near.append(row)

    loads[2 + CH].wait()

    def back_step(n, total):
        cols = pl.ds(pl.multiple_of(n * 512, 512), 512)
        return total + lax.dot_general(
            w[:, cols], og[:, cols], (((1,), (1,)), ((), ())), preferred_element_type=F32
        )

    back = lax.fori_loop(0, D // 512, back_step, jnp.zeros((ROWS, TOK), F32))
    hg_ref[...] = (back * D ** (-0.5)).astype(BF16)

    group = pl.ds(pl.multiple_of(g * 4 * J, 64), 4 * J)
    far_c = []
    for ch in range(CH):
        total = full[ch, group, :]
        for k in range(7):
            near[ch][k].wait_recv()
            total = total + in1[ch, k].astype(F32)
        acc1[ch] = total
        t2[ch] = total.astype(BF16)
        row = []
        for d in (1, 2, 3):
            src = t2.at[ch, pl.ds(pl.multiple_of(((a + d) % 4) * J, J), J)]
            row.append(
                start(remote(src, in2.at[ch, d - 1], s2.at[ch, d - 1], r2.at[ch, d - 1], far[d - 1]))
            )
        far_c.append(row)

    steps = jnp.full((J, 128), step_ref[0], jnp.int32)
    pow1 = jnp.full((J, 128), 1.0, F32)
    pow2 = pow1
    for n in range(1, 9):
        pow1 = pow1 * jnp.where(steps >= n, 0.9, 1.0).astype(F32)
        pow2 = pow2 * jnp.where(steps >= n, 0.95, 1.0).astype(F32)
    fix1, fix2 = 1.0 - pow1, 1.0 - pow2

    own_rows = pl.ds(pl.multiple_of((c * 32 + g * 4 + a) * J, J), J)
    for x in loads[3 + CH :]:
        x.wait()
    first_c = []
    for ch in range(CH):
        grads = acc1[ch, pl.ds(pl.multiple_of(a * J, J), J), :]
        for d in range(3):
            far_c[ch][d].wait_recv()
            grads = grads + in2[ch, d].astype(F32)
        grads = grads * (1.0 / TOK)
        at_rows = pl.ds(ch * J, J)
        master = m_ref[at_rows, :]
        new_f = 0.9 * f_ref[at_rows, :] + 0.1 * grads
        new_s = 0.95 * s_ref[at_rows, :] + 0.05 * grads * grads
        update = new_f / fix1 / (jnp.sqrt(new_s / fix2) + 1e-08)
        new_m = master - 0.05 * (update + 0.1 * master)
        ag[ch, own_rows, :] = new_m.astype(BF16)
        row = []
        for d in range(3):
            here = ag.at[ch, own_rows]
            row.append(start(remote(here, here, sa.at[ch, d], ra.at[ch, d], far[d])))
        first_c.append(row)
        nm_ref[at_rows, :] = new_m
        nf_ref[at_rows, :] = new_f
        ns_ref[at_rows, :] = new_s
        moved[0, at_rows, :] = new_m
        moved[1, at_rows, :] = new_f
        moved[2, at_rows, :] = new_s

    mine_g = pl.ds(pl.multiple_of((c * 8 + g) * 4 * J, 64), 4 * J)
    second_c = []
    for ch in range(CH):
        for d in range(3):
            first_c[ch][d].wait_recv()
        row = []
        for k in range(7):
            here = ag.at[ch, mine_g]
            row.append(start(remote(here, here, sb.at[ch, k], rb.at[ch, k], near_to[k])))
        second_c.append(row)
    ck = start(remote(moved, ck_ref, sk, rk, nxt))

    half = pl.ds(pl.multiple_of(c * 32 * J, 512), 32 * J)
    third_c = []
    for ch in range(CH):
        for k in range(7):
            second_c[ch][k].wait_recv()
        here = ag.at[ch, half]
        third_c.append(start(remote(here, here, sc.at[ch], rc.at[ch], sib)))
    for ch in range(CH):
        third_c[ch].wait_recv()
        wide[ch] = ag[ch].astype(F32)
        for n in range(J // 4):
            rows = [
                wide[ch, pl.ds(4 * n + q, ROWS, stride=J), :].astype(BF16) for q in range(4)
            ]
            wn_ref[:, pl.ds(ch * W + n * 512, 512)] = jnp.dot(
                at, jnp.concatenate(rows, axis=1), preferred_element_type=F32
            ).astype(BF16)
    ck.wait_recv()
    for copy in sends:
        copy.wait_send()


def per_device(
    hidden, out_grad, weights_old, master, first_moment, second_moment, owner_order, step_count
):
    vmem = pl.BlockSpec(memory_space=pltpu.VMEM)
    hbm = pl.BlockSpec(memory_space=pltpu.HBM)
    own = jax.ShapeDtypeStruct((48, 128), F32)
    dma = pltpu.SemaphoreType.DMA
    nm, nf, ns, ck, wn, hg = pl.pallas_call(
        kernel,
        out_shape=(
            own, own, own,
            jax.ShapeDtypeStruct((3, 48, 128), F32),
            jax.ShapeDtypeStruct((ROWS, D), BF16),
            jax.ShapeDtypeStruct((ROWS, TOK), BF16),
        ),
        in_specs=[
            hbm, hbm, pl.BlockSpec(memory_space=pltpu.SMEM), hbm, hbm, hbm, hbm, hbm,
        ],
        out_specs=(vmem,) * 6,
        scratch_shapes=[
            pltpu.VMEM((ROWS, TOK), BF16),
            pltpu.VMEM((1, ROWS), jnp.int32),
            pltpu.VMEM((48, 128), F32),
            pltpu.VMEM((48, 128), F32),
            pltpu.VMEM((48, 128), F32),
            pltpu.VMEM((TOK, D), BF16),
            pltpu.VMEM((ROWS, D), BF16),
            pltpu.VMEM((CH, ROWS, W), F32),
            pltpu.VMEM((CH, 32, W), F32),
            pltpu.VMEM((CH, 32 * J, 128), F32),
            pltpu.VMEM((CH, 32 * J, 128), BF16),
            pltpu.VMEM((CH, 7, 4 * J, 128), BF16),
            pltpu.VMEM((CH, 4 * J, 128), F32),
            pltpu.VMEM((CH, 4 * J, 128), BF16),
            pltpu.VMEM((CH, 3, J, 128), BF16),
            pltpu.VMEM((CH, 64 * J, 128), BF16),
            pltpu.VMEM((CH, 64 * J, 128), F32),
            pltpu.VMEM((3, 48, 128), F32),
            dma((CH + 6,)),
            dma((CH,)), dma((CH,)),
            dma((CH, 7)), dma((CH, 7)),
            dma((CH, 3)), dma((CH, 3)),
            dma((CH, 3)), dma((CH, 3)),
            dma((CH, 7)), dma((CH, 7)),
            dma((CH,)), dma((CH,)),
            dma, dma,
        ],
        compiler_params=pltpu.CompilerParams(
            collective_id=0, has_side_effects=True, vmem_limit_bytes=60 * 1024 * 1024
        ),
        cost_estimate=pl.CostEstimate(
            flops=4 * ROWS * TOK * D, bytes_accessed=6 * 1024 * 1024, transcendentals=0
        ),
    )(
        hidden[0].T,
        owner_order.reshape(1, ROWS),
        step_count,
        out_grad[0],
        weights_old,
        master.reshape(48, 128),
        first_moment.reshape(48, 128),
        second_moment.reshape(48, 128),
    )
    return (
        nm.reshape(1, D), nf.reshape(1, D), ns.reshape(1, D),
        ck.reshape(3, 1, D), wn, hg.T[None],
    )


def solution(mesh):
    placed = (
        P("section", "replica", None),
        P("section", "replica", None),
        P("section", None),
        P(("section", "replica"), None),
        P(("section", "replica"), None),
        P(("section", "replica"), None),
        P(),
        P(),
    )
    return jax.shard_map(
        per_device,
        mesh=mesh,
        in_specs=placed,
        out_specs=(
            P(("section", "replica"), None),
            P(("section", "replica"), None),
            P(("section", "replica"), None),
            P(None, ("section", "replica"), None),
            P("section", None),
            P("section", "replica", None),
        ),
        check_vma=False,
    )
```

time: 190 us -> 63.7 us (0.34)
  waiting for transfers between devices: 104 us -> 0 us
  Pallas kernels: 0 us -> 53 us
  starting transfers between devices: 41.7 us -> 0 us
  other arithmetic: 14.4 us -> 0 us
  local copies, waits for them, and re-layouts: 23.2 us -> 9 us
  matrix products: 3.54 us -> 0 us
    all_to_all x2 -> x0, waiting for transfers between devices: 103 us -> none  [the longest x1 75.6 us: sent_and_summed(): lax.all_to_all(cut_along(array, dim, devices), axis, 0, 0, tiled=True)]
    pallas_call x0 -> x1, Pallas kernels: none -> 53 us  [per_device(): pl.pallas_call(kernel, out_shape=(own, own, own, jax.ShapeDtypeStruct((3,...]
    all_to_all x2 -> x0, starting transfers between devices: 31.3 us -> none  [the longest x1 23.4 us: sent_and_summed(): lax.all_to_all(cut_along(array, dim, devices), axis, 0, 0, tiled=True)]
    ppermute x3 -> x0, starting transfers between devices: 10.4 us -> none  [passed_along(): lax.ppermute(array, axis, [(i, (i + by) % devices) for i in range(devices)])]
    broadcast_in_dim x1 -> x0, other arithmetic: 7.28 us -> none  [from_everyone(): copies = jnp.broadcast_to(array, (lax.axis_size(axis), *array.shape))]
    gather x2 -> x0, local copies, waits for them, and re-layouts: 5.31 us -> none  [the longest x1 3.89 us: per_device(): jnp.take(gathered.reshape(replicas, block, width), inverse, axis=0)]
    dot_general x2 -> x0, matrix products: 3.54 us -> none  [the longest x1 2.83 us: per_device(): lax.dot_general(grads_out, weights_old, (((1,), (1,)), ((), ())), preferr...]
    select_n x3 -> x0, other arithmetic: 2.97 us -> none  [the longest x2 2.16 us: per_device(): jnp.take(gathered.reshape(replicas, block, width), inverse, axis=0)]
  transfers between devices with their start and end apart: 5 -> 0, of which waited for: 3 -> 0; matrix products, arithmetic and copies ran while one was open for 2% -> 0% of each run, Pallas kernels for 0% -> 0%
where the time goes in v1:
time: 63.7 us; the launch traced here: 63.3 us
  Pallas kernels  53 us (83%)
  local copies, waits for them, and re-layouts  9 us (14%)
  between operations  1.29 us (2%)
    pallas_call x1, Pallas kernels, per_device(): pl.pallas_call(kernel, out_shape=(own, own, own, jax.ShapeDtypeStruct((3,...  53 us
    unnamed x6, local copies, waits for them, and re-layouts  9 us

profile of v1, /device:TPU:1, one launch (start us, length us, event | category | flops | bytes accessed | tf_op | source)
XLA Modules:
  0.0 63.3 jit_solution(10131797862016251292)
XLA Ops:
  1.3 53.0 %shard_map.127 = (f32[48,128]{1,0:T(8,128)}, f32[48,128]{1,0:T(8,128)}, f32[48,128]{1,0:T(8,128)}, f32[3,48,128]{2,1,0:T(8,128)}, bf16[64,6144]{1,0:T(8,128)(2,1)}, /*index=5*/bf16[64,256]{1,0:T(8,128)(2,1)}) custom-call(bf16[64,256]{1,0:T(8,128)(2,1)} %bitcast.17, s32[1,64]{1,0:T(1,128)} %bitcast.25, s32[1]{0:T(128)S(6)} %copy.22.step_ref, ...), custom_call_target="tpu_custom_call" | custom-call | flops 402653184 | bytes 6291456 | tf_op jit(solution)/shard_map/pallas_call | solution.py:227
  54.3 1.3 %copy.23 = f32[1,6144]{1,0:T(1,128)} copy(f32[1,6144]{1,0:T(1,128)} %bitcast.24) | data formatting | bytes 49152
  55.6 1.3 %copy.24 = f32[1,6144]{1,0:T(1,128)} copy(f32[1,6144]{1,0:T(1,128)} %bitcast.23) | data formatting | bytes 49152
  56.9 1.3 %copy.25 = f32[1,6144]{1,0:T(1,128)} copy(f32[1,6144]{1,0:T(1,128)} %bitcast.22) | data formatting | bytes 49152
  58.3 1.5 %copy.26 = f32[3,1,6144]{2,1,0:T(1,128)} copy(f32[3,1,6144]{2,1,0:T(1,128)} %bitcast.16) | data formatting | bytes 147456
  59.8 2.1 %copy.27 = bf16[64,6144]{1,0:T(8,128)(2,1)} copy(bf16[64,6144]{1,0:T(8,128)(2,1)} %get-tuple-element.40) | data formatting | bytes 1572864
  61.9 1.4 %copy.28 = bf16[1,256,64]{1,2,0:T(8,128)(2,1)} copy(bf16[1,256,64]{1,2,0:T(8,128)(2,1)} %bitcast.18) | data formatting | bytes 65536

commit v2 on v1

--- a/solution.py
+++ b/solution.py
@@ -202,9 +202,12 @@
             second_c[ch][k].wait_recv()
         here = ag.at[ch, half]
         third_c.append(start(remote(here, here, sc.at[ch], rc.at[ch], sib)))
+    other = pl.ds(pl.multiple_of((1 - c) * 32 * J, 512), 32 * J)
+    for ch in range(CH):
+        wide[ch, half, :] = ag[ch, half, :].astype(F32)
     for ch in range(CH):
         third_c[ch].wait_recv()
-        wide[ch] = ag[ch].astype(F32)
+        wide[ch, other, :] = ag[ch, other, :].astype(F32)
         for n in range(J // 4):
             rows = [
                 wide[ch, pl.ds(4 * n + q, ROWS, stride=J), :].astype(BF16) for q in range(4)
@@ -217,20 +220,29 @@
         copy.wait_send()
 
 
+def write_out(*refs):
+    srcs, dsts, sems = refs[:6], refs[6:12], refs[12]
+    copies = [pltpu.make_async_copy(a, b, sems.at[i]) for i, (a, b) in enumerate(zip(srcs, dsts))]
+    for x in copies:
+        x.start()
+    for x in copies:
+        x.wait()
+
+
 def per_device(
     hidden, out_grad, weights_old, master, first_moment, second_moment, owner_order, step_count
 ):
     vmem = pl.BlockSpec(memory_space=pltpu.VMEM)
     hbm = pl.BlockSpec(memory_space=pltpu.HBM)
-    own = jax.ShapeDtypeStruct((48, 128), F32)
+    own = pltpu.VMEM((48, 128), F32)
     dma = pltpu.SemaphoreType.DMA
     nm, nf, ns, ck, wn, hg = pl.pallas_call(
         kernel,
         out_shape=(
             own, own, own,
-            jax.ShapeDtypeStruct((3, 48, 128), F32),
-            jax.ShapeDtypeStruct((ROWS, D), BF16),
-            jax.ShapeDtypeStruct((ROWS, TOK), BF16),
+            pltpu.VMEM((3, 48, 128), F32),
+            pltpu.VMEM((ROWS, D), BF16),
+            pltpu.VMEM((ROWS, TOK), BF16),
         ),
         in_specs=[
             hbm, hbm, pl.BlockSpec(memory_space=pltpu.SMEM), hbm, hbm, hbm, hbm, hbm,
@@ -280,6 +292,14 @@
         first_moment.reshape(48, 128),
         second_moment.reshape(48, 128),
     )
+    nm, nf, ns, ck, wn, hg = pl.pallas_call(
+        write_out,
+        out_shape=[jax.ShapeDtypeStruct(x.shape, x.dtype) for x in (nm, nf, ns, ck, wn, hg)],
+        in_specs=[vmem] * 6,
+        out_specs=[hbm] * 6,
+        scratch_shapes=[dma((6,))],
+        compiler_params=pltpu.CompilerParams(vmem_limit_bytes=2 * 1024 * 1024),
+    )(nm, nf, ns, ck, wn, hg)
     return (
         nm.reshape(1, D), nf.reshape(1, D), ns.reshape(1, D),
         ck.reshape(3, 1, D), wn, hg.T[None],

time: 63.7 us -> 54.5 us (0.86)
  local copies, waits for them, and re-layouts: 9 us -> 0 us
    unnamed x6 -> x0, local copies, waits for them, and re-layouts: 9 us -> none
    pallas_call x1 -> x2, Pallas kernels: 53 us -> 53 us  [the longest x1 52.1 us: per_device(): pl.pallas_call(kernel, out_shape=(own, own, own, pltpu.VMEM((3, 48, 128),...]
where the time goes in v2:
time: 54.5 us; the launch traced here: 54.3 us
  Pallas kernels  53 us (97%)
  between operations  1.29 us (2%)
    pallas_call x1, Pallas kernels, per_device(): pl.pallas_call(kernel, out_shape=(own, own, own, pltpu.VMEM((3, 48, 128),...  52.1 us

profile of v2, /device:TPU:1, one launch (start us, length us, event | category | flops | bytes accessed | tf_op | source)
XLA Modules:
  0.0 54.3 jit_solution(611678372518657876)
XLA Ops:
  1.3 52.1 %shard_map.127 = (f32[48,128]{1,0:T(8,128)S(1)}, f32[48,128]{1,0:T(8,128)S(1)}, f32[48,128]{1,0:T(8,128)S(1)}, f32[3,48,128]{2,1,0:T(8,128)S(1)}, bf16[64,6144]{...) custom-call(bf16[64,256]{1,0:T(8,128)(2,1)} %bitcast.16, s32[1,64]{1,0:T(1,128)} %bitcast.20, s32[1]{0:T(128)S(6)} %copy.16.step_ref, ...), custom_call_target="tpu_custom_call" | custom-call | flops 402653184 | bytes 6291456 | tf_op jit(solution)/shard_map/pallas_call | solution.py:239
  53.3 1.0 %shard_map.128 = (f32[48,128]{1,0:T(8,128)}, f32[48,128]{1,0:T(8,128)}, f32[48,128]{1,0:T(8,128)}, f32[3,48,128]{2,1,0:T(8,128)}, bf16[64,6144]{1,0:T(8,128)(2,1)}, /*index=5*/bf16[64,256]{1,0:T(8,128)(2,1)}) custom-call(f32[48,128]{1,0:T(8,128)S(1)} %get-tuple-element.18.refs_0_, f32[48,128]{1,0:T(8,128)S(1)} %get-tuple-element.19.refs_1_, ...), custom_call_target="tpu_custom_call" | custom-call | tf_op jit(solution)/shard_map/pallas_call | solution.py:295

commit v3 on v2

--- a/solution.py
+++ b/solution.py
@@ -15,6 +15,7 @@
 CH = 3
 W = D // CH
 J = W // 128
+FAR = (6, -6, 2, -2)
 FLIPS = [(i, f) for f in (1, 0) for i in range(4) if (i, f) != (0, 0)]
 
 
@@ -26,13 +27,13 @@
 def kernel(
     hid_hbm, own_hbm, step_ref, og_hbm, w_hbm, m_hbm, f_hbm, s_hbm,
     nm_ref, nf_ref, ns_ref, ck_ref, wn_ref, hg_ref,
-    hid_ref, own_ref, m_ref, f_ref, s_ref, og, w, part, core_in, full, t1, in1, acc1, t2, in2, ag, wide, moved,
+    hid_ref, own_ref, m_ref, f_ref, s_ref, og, w, part, core_in, full, t1, in1, t2, in2, fresh, ag, wide, moved,
     ld_sem, core_s, core_r, s1, r1, s2, r2, sa, ra, sb, rb, sc, rc, sk, rk,
 ):
     r = lax.axis_index("replica")
     z, xh, c = r // 4, (r // 2) % 2, r % 2
     a, zl = z // 4, z % 4
-    g = xh * 4 + zl
+    g = xh * 4 + (z + 2) % 4
 
     def rep(z_, x_, c_):
         return ((z_ + 32) % 16) * 4 + x_ * 2 + c_
@@ -42,7 +43,7 @@
     nxt, prv = (r + 1) % 64, (r + 63) % 64
     near_to = [(rep(z + offs[i], (xh + f) % 2, c)) for i, f in FLIPS]
     near_from = [(rep(z - offs[i], (xh + f) % 2, c)) for i, f in FLIPS]
-    far = [rep(z + 4 * d, xh, c) for d in (1, 2, 3)]
+    far = [rep(z + d, xh, c) for d in FAR]
 
     def remote(src, dst, ssem, rsem, to):
         return pltpu.make_async_remote_copy(
@@ -99,7 +100,7 @@
                 hid, og[:, at_col : at_col + 512], preferred_element_type=F32
             )
         if ch == 0:
-            pl.semaphore_wait(barrier, 12)
+            pl.semaphore_wait(barrier, 13)
         core.append(
             start(remote(part.at[ch, theirs], core_in.at[ch], core_s.at[ch], core_r.at[ch], sib))
         )
@@ -113,7 +114,7 @@
         t1[ch] = full[ch].astype(BF16)
         row = []
         for k, (i, f) in enumerate(FLIPS):
-            there = ((xh + f) % 2) * 4 + (z + offs[i] + 16) % 4
+            there = ((xh + f) % 2) * 4 + (z + offs[i] + 18) % 4
             src = t1.at[ch, pl.ds(pl.multiple_of(there * 4 * J, 64), 4 * J)]
             row.append(start(remote(src, in1.at[ch, k], s1.at[ch, k], r1.at[ch, k], near_to[k])))
         near.append(row)
@@ -136,14 +137,12 @@
         for k in range(7):
             near[ch][k].wait_recv()
             total = total + in1[ch, k].astype(F32)
-        acc1[ch] = total
         t2[ch] = total.astype(BF16)
         row = []
-        for d in (1, 2, 3):
-            src = t2.at[ch, pl.ds(pl.multiple_of(((a + d) % 4) * J, J), J)]
-            row.append(
-                start(remote(src, in2.at[ch, d - 1], s2.at[ch, d - 1], r2.at[ch, d - 1], far[d - 1]))
-            )
+        for d in range(4):
+            block = ((z + FAR[d] + 16) % 16) // 4
+            src = t2.at[ch, pl.ds(pl.multiple_of(block * J, J), J)]
+            row.append(start(remote(src, in2.at[ch, d], s2.at[ch, d], r2.at[ch, d], far[d])))
         far_c.append(row)
 
     steps = jnp.full((J, 128), step_ref[0], jnp.int32)
@@ -154,15 +153,15 @@
         pow2 = pow2 * jnp.where(steps >= n, 0.95, 1.0).astype(F32)
     fix1, fix2 = 1.0 - pow1, 1.0 - pow2
 
-    own_rows = pl.ds(pl.multiple_of((c * 32 + g * 4 + a) * J, J), J)
+    own_rows = pl.ds(pl.multiple_of((c * 32 + xh * 16 + zl * 4 + a) * J, J), J)
     for x in loads[3 + CH :]:
         x.wait()
     first_c = []
     for ch in range(CH):
-        grads = acc1[ch, pl.ds(pl.multiple_of(a * J, J), J), :]
-        for d in range(3):
+        for d in range(4):
             far_c[ch][d].wait_recv()
-            grads = grads + in2[ch, d].astype(F32)
+        grads = in2[ch, 0].astype(F32) + in2[ch, 1].astype(F32)
+        grads = grads + in2[ch, 2].astype(F32) + in2[ch, 3].astype(F32)
         grads = grads * (1.0 / TOK)
         at_rows = pl.ds(ch * J, J)
         master = m_ref[at_rows, :]
@@ -170,11 +169,11 @@
         new_s = 0.95 * s_ref[at_rows, :] + 0.05 * grads * grads
         update = new_f / fix1 / (jnp.sqrt(new_s / fix2) + 1e-08)
         new_m = master - 0.05 * (update + 0.1 * master)
-        ag[ch, own_rows, :] = new_m.astype(BF16)
+        fresh[ch] = new_m.astype(BF16)
         row = []
-        for d in range(3):
-            here = ag.at[ch, own_rows]
-            row.append(start(remote(here, here, sa.at[ch, d], ra.at[ch, d], far[d])))
+        for d in range(4):
+            there = ag.at[ch, own_rows]
+            row.append(start(remote(fresh.at[ch], there, sa.at[ch, d], ra.at[ch, d], far[d])))
         first_c.append(row)
         nm_ref[at_rows, :] = new_m
         nf_ref[at_rows, :] = new_f
@@ -186,7 +185,7 @@
     mine_g = pl.ds(pl.multiple_of((c * 8 + g) * 4 * J, 64), 4 * J)
     second_c = []
     for ch in range(CH):
-        for d in range(3):
+        for d in range(4):
             first_c[ch][d].wait_recv()
         row = []
         for k in range(7):
@@ -261,17 +260,17 @@
             pltpu.VMEM((CH, 32 * J, 128), F32),
             pltpu.VMEM((CH, 32 * J, 128), BF16),
             pltpu.VMEM((CH, 7, 4 * J, 128), BF16),
-            pltpu.VMEM((CH, 4 * J, 128), F32),
             pltpu.VMEM((CH, 4 * J, 128), BF16),
-            pltpu.VMEM((CH, 3, J, 128), BF16),
+            pltpu.VMEM((CH, 4, J, 128), BF16),
+            pltpu.VMEM((CH, J, 128), BF16),
             pltpu.VMEM((CH, 64 * J, 128), BF16),
             pltpu.VMEM((CH, 64 * J, 128), F32),
             pltpu.VMEM((3, 48, 128), F32),
             dma((CH + 6,)),
             dma((CH,)), dma((CH,)),
             dma((CH, 7)), dma((CH, 7)),
-            dma((CH, 3)), dma((CH, 3)),
-            dma((CH, 3)), dma((CH, 3)),
+            dma((CH, 4)), dma((CH, 4)),
+            dma((CH, 4)), dma((CH, 4)),
             dma((CH, 7)), dma((CH, 7)),
             dma((CH,)), dma((CH,)),
             dma, dma,

time: 54.5 us -> 52.7 us (0.967)
  Pallas kernels: 53 us -> 51.3 us
    pallas_call x1, Pallas kernels: 52.1 us -> 50.3 us  [per_device(): pl.pallas_call(kernel, out_shape=(own, own, own, pltpu.VMEM((3, 48, 128),...]
where the time goes in v3:
time: 52.7 us; the launch traced here: 52.6 us
  Pallas kernels  51.3 us (97%)
  between operations  1.29 us (2%)
    pallas_call x1, Pallas kernels, per_device(): pl.pallas_call(kernel, out_shape=(own, own, own, pltpu.VMEM((3, 48, 128),...  50.3 us

profile of v3, /device:TPU:1, one launch (start us, length us, event | category | flops | bytes accessed | tf_op | source)
XLA Modules:
  0.0 52.6 jit_solution(9998730998693728469)
XLA Ops:
  1.3 50.3 %shard_map.127 = (f32[48,128]{1,0:T(8,128)S(1)}, f32[48,128]{1,0:T(8,128)S(1)}, f32[48,128]{1,0:T(8,128)S(1)}, f32[3,48,128]{2,1,0:T(8,128)S(1)}, bf16[64,6144]{...) custom-call(bf16[64,256]{1,0:T(8,128)(2,1)} %bitcast.16, s32[1,64]{1,0:T(1,128)} %bitcast.20, s32[1]{0:T(128)S(6)} %copy.16.step_ref, ...), custom_call_target="tpu_custom_call" | custom-call | flops 402653184 | bytes 6291456 | tf_op jit(solution)/shard_map/pallas_call | solution.py:238
  51.6 1.0 %shard_map.128 = (f32[48,128]{1,0:T(8,128)}, f32[48,128]{1,0:T(8,128)}, f32[48,128]{1,0:T(8,128)}, f32[3,48,128]{2,1,0:T(8,128)}, bf16[64,6144]{1,0:T(8,128)(2,1)}, /*index=5*/bf16[64,256]{1,0:T(8,128)(2,1)}) custom-call(f32[48,128]{1,0:T(8,128)S(1)} %get-tuple-element.18.refs_0_, f32[48,128]{1,0:T(8,128)S(1)} %get-tuple-element.19.refs_1_, ...), custom_call_target="tpu_custom_call" | custom-call | tf_op jit(solution)/shard_map/pallas_call | solution.py:294

commit v4 on v3

--- a/solution.py
+++ b/solution.py
@@ -16,7 +16,7 @@
 W = D // CH
 J = W // 128
 FAR = (6, -6, 2, -2)
-FLIPS = [(i, f) for f in (1, 0) for i in range(4) if (i, f) != (0, 0)]
+FLIPS = [(i, f) for i in (3, 2, 1, 0) for f in (1, 0) if (i, f) != (0, 0)]
 
 
 def rep_of(p):
@@ -182,6 +182,7 @@
         moved[1, at_rows, :] = new_f
         moved[2, at_rows, :] = new_s
 
+    ck = start(remote(moved, ck_ref, sk, rk, nxt))
     mine_g = pl.ds(pl.multiple_of((c * 8 + g) * 4 * J, 64), 4 * J)
     second_c = []
     for ch in range(CH):
@@ -192,7 +193,6 @@
             here = ag.at[ch, mine_g]
             row.append(start(remote(here, here, sb.at[ch, k], rb.at[ch, k], near_to[k])))
         second_c.append(row)
-    ck = start(remote(moved, ck_ref, sk, rk, nxt))
 
     half = pl.ds(pl.multiple_of(c * 32 * J, 512), 32 * J)
     third_c = []

time: 52.7 us -> 52.2 us (level)
  no operation moved by 1% of the time
where the time goes in v4:
time: 52.2 us; the launch traced here: 52.1 us
  Pallas kernels  50.8 us (97%)
  between operations  1.29 us (2%)
    pallas_call x1, Pallas kernels, per_device(): pl.pallas_call(kernel, out_shape=(own, own, own, pltpu.VMEM((3, 48, 128),...  49.8 us

profile of v4, /device:TPU:1, one launch (start us, length us, event | category | flops | bytes accessed | tf_op | source)
XLA Modules:
  0.0 52.1 jit_solution(17085560579619758945)
XLA Ops:
  1.3 49.8 %shard_map.127 = (f32[48,128]{1,0:T(8,128)S(1)}, f32[48,128]{1,0:T(8,128)S(1)}, f32[48,128]{1,0:T(8,128)S(1)}, f32[3,48,128]{2,1,0:T(8,128)S(1)}, bf16[64,6144]{...) custom-call(bf16[64,256]{1,0:T(8,128)(2,1)} %bitcast.16, s32[1,64]{1,0:T(1,128)} %bitcast.20, s32[1]{0:T(128)S(6)} %copy.16.step_ref, ...), custom_call_target="tpu_custom_call" | custom-call | flops 402653184 | bytes 6291456 | tf_op jit(solution)/shard_map/pallas_call | solution.py:238
  51.1 1.0 %shard_map.128 = (f32[48,128]{1,0:T(8,128)}, f32[48,128]{1,0:T(8,128)}, f32[48,128]{1,0:T(8,128)}, f32[3,48,128]{2,1,0:T(8,128)}, bf16[64,6144]{1,0:T(8,128)(2,1)}, /*index=5*/bf16[64,256]{1,0:T(8,128)(2,1)}) custom-call(f32[48,128]{1,0:T(8,128)S(1)} %get-tuple-element.18.refs_0_, f32[48,128]{1,0:T(8,128)S(1)} %get-tuple-element.19.refs_1_, ...), custom_call_target="tpu_custom_call" | custom-call | tf_op jit(solution)/shard_map/pallas_call | solution.py:294

commit v5 on v4

--- a/solution.py
+++ b/solution.py
@@ -83,6 +83,7 @@
     ).astype(BF16)
 
     sends = []
+    gone = []
 
     def start(copy):
         copy.start()
@@ -156,6 +157,8 @@
     own_rows = pl.ds(pl.multiple_of((c * 32 + xh * 16 + zl * 4 + a) * J, J), J)
     for x in loads[3 + CH :]:
         x.wait()
+    gone += sends
+    sends.clear()
     first_c = []
     for ch in range(CH):
         for d in range(4):
@@ -183,6 +186,8 @@
         moved[2, at_rows, :] = new_s
 
     ck = start(remote(moved, ck_ref, sk, rk, nxt))
+    for copy in gone:
+        copy.wait_send()
     mine_g = pl.ds(pl.multiple_of((c * 8 + g) * 4 * J, 64), 4 * J)
     second_c = []
     for ch in range(CH):
@@ -201,6 +206,8 @@
             second_c[ch][k].wait_recv()
         here = ag.at[ch, half]
         third_c.append(start(remote(here, here, sc.at[ch], rc.at[ch], sib)))
+    for copy in sends[:-CH]:
+        copy.wait_send()
     other = pl.ds(pl.multiple_of((1 - c) * 32 * J, 512), 32 * J)
     for ch in range(CH):
         wide[ch, half, :] = ag[ch, half, :].astype(F32)
@@ -215,7 +222,7 @@
                 at, jnp.concatenate(rows, axis=1), preferred_element_type=F32
             ).astype(BF16)
     ck.wait_recv()
-    for copy in sends:
+    for copy in sends[-CH:]:
         copy.wait_send()
 
 

time: 52.2 us -> 52.1 us (level)
  no operation moved by 1% of the time
where the time goes in v5:
time: 52.1 us; the launch traced here: 52 us
  Pallas kernels  50.7 us (97%)
  between operations  1.29 us (2%)
    pallas_call x1, Pallas kernels, per_device(): pl.pallas_call(kernel, out_shape=(own, own, own, pltpu.VMEM((3, 48, 128),...  49.7 us

profile of v5, /device:TPU:1, one launch (start us, length us, event | category | flops | bytes accessed | tf_op | source)
XLA Modules:
  0.0 52.0 jit_solution(5897202001069931952)
XLA Ops:
  1.3 49.7 %shard_map.127 = (f32[48,128]{1,0:T(8,128)S(1)}, f32[48,128]{1,0:T(8,128)S(1)}, f32[48,128]{1,0:T(8,128)S(1)}, f32[3,48,128]{2,1,0:T(8,128)S(1)}, bf16[64,6144]{...) custom-call(bf16[64,256]{1,0:T(8,128)(2,1)} %bitcast.16, s32[1,64]{1,0:T(1,128)} %bitcast.20, s32[1]{0:T(128)S(6)} %copy.16.step_ref, ...), custom_call_target="tpu_custom_call" | custom-call | flops 402653184 | bytes 6291456 | tf_op jit(solution)/shard_map/pallas_call | solution.py:245
  51.0 1.0 %shard_map.128 = (f32[48,128]{1,0:T(8,128)}, f32[48,128]{1,0:T(8,128)}, f32[48,128]{1,0:T(8,128)}, f32[3,48,128]{2,1,0:T(8,128)}, bf16[64,6144]{1,0:T(8,128)(2,1)}, /*index=5*/bf16[64,256]{1,0:T(8,128)(2,1)}) custom-call(f32[48,128]{1,0:T(8,128)S(1)} %get-tuple-element.18.refs_0_, f32[48,128]{1,0:T(8,128)S(1)} %get-tuple-element.19.refs_1_, ...), custom_call_target="tpu_custom_call" | custom-call | tf_op jit(solution)/shard_map/pallas_call | solution.py:301
